TPU v7x, 32 devices: a whole 2x2x4 slice. The times are simulated.
32 devices in a mesh: seq: 8 (over y, x, core), head: 4 (over z).
Axes of the slice: x: 2, y: 2, z: 4, core: 2. Of those that a mesh axis runs over, the one named last changes fastest.
Arguments:
- query_vectors: bfloat16 [4096, 4096], P('seq', 'head'), may hold values from -4.375 to 4.375
- key_vectors: bfloat16 [4096, 4096], P('seq', 'head'), may hold values from -4.375 to 4.375
- value_vectors: bfloat16 [4096, 4096], P('seq', 'head'), may hold values from -8 to 8
- upstream: bfloat16 [4096, 4096], P('seq', 'head'), may hold values from -6 to 6
- out_weight: bfloat16 [4096, 4096], P('head', 'seq'), may hold values from -0.09375 to 0.09375
- gate_logit: float32 [32], P('head'), may hold values from -2 to 2
- document_ids: int32 [8], replicated, may hold values from 0 to 2, as said below
- valid_lengths: int32 [8], replicated, may hold values from 64 to 512, as said below
Outputs:
- mixed: bfloat16 [4096, 4096], P('seq', 'head')
- grad_queries: bfloat16 [4096, 4096], P('seq', 'head')
- grad_keys: bfloat16 [4096, 4096], P('seq', 'head')
- grad_values: bfloat16 [4096, 4096], P('seq', 'head')
Inputs may be any that keep to these rules, and one draw needn't show every extreme that they name: `document_ids`: never falling; every document spans 1 to 4 consecutive segments, and one spans exactly 4. `valid_lengths`: every segment but the last of its document is full; the last segment of some document holds 64 tokens.
All inputs are finite; a program needn't handle non-finite values.
Results may differ from a plain program's by a relative error of at most 0.012.
Values may be sent and summed in bfloat16 or wider, within the bound.
A program may use at most 128 MiB of HBM per device.

v0:
```python
import functools

import jax
import jax.numpy as jnp
from jax import lax
from jax.experimental import pallas as pl
from jax.experimental.pallas import tpu as pltpu
from jax.sharding import PartitionSpec as P

F32 = jnp.float32
BF16 = jnp.bfloat16
EXT = 16
PARAMS = pltpu.CompilerParams(vmem_limit_bytes=40 * 1024 * 1024)

SMEM = pl.BlockSpec(memory_space=pltpu.SMEM)


def lift(x):
    return jnp.where(x > 0, x + 1.0, jnp.exp(jnp.minimum(x, 0.0)))


def lift_slope(x):
    return jnp.where(x > 0, 1.0, jnp.exp(jnp.minimum(x, 0.0)))


def dot(a, b, ca, cb):
    return lax.dot_general(a, b, (((ca,), (cb,)), ((), ())), preferred_element_type=F32)


def row_mask(rows, valid, first=0):
    return lax.broadcasted_iota(jnp.int32, (rows, 1), 0) + first < valid


def with_ones(v):
    return jnp.concatenate([v, jnp.ones((v.shape[0], EXT), v.dtype)], axis=1)


def state_kernel(valid_ref, k_ref, v_ref, out_ref):
    seg, hd = k_ref.shape
    live = row_mask(seg, valid_ref[0])
    lifted = jnp.where(live, lift(k_ref[...].astype(F32)), 0.0).astype(BF16)
    out_ref[0] = dot(with_ones(v_ref[...]), lifted, 0, 0).astype(BF16)


def total_state(weight_ref, all_ref):
    total = jnp.zeros(all_ref.shape[2:], F32)
    for t in range(all_ref.shape[0]):
        total = total + jnp.where(weight_ref[t] > 0, all_ref[t, 0].astype(F32), 0.0)
    return total


def forward_kernel(valid_ref, weight_ref, gate_ref, q_ref, k_ref, v_ref, all_ref, attn_ref, p_ref, mem_ref):
    seg, hd = q_ref.shape
    half = seg // 2
    valid = valid_ref[0]
    gate = gate_ref[pl.program_id(0)]
    mem = total_state(weight_ref, all_ref).astype(BF16)
    mem_ref[0] = mem
    scale = hd ** -0.5
    lifted = lift(q_ref[...].astype(F32)).astype(BF16)
    recall = dot(lifted, mem, 1, 1)
    recalled = recall[:, :hd] / (1.0 + recall[:, hd:hd + 1])
    p_ref[0, :half, half:] = jnp.zeros((half, seg - half), BF16)
    for first, count in ((0, half), (half, seg)):
        rows = slice(first, first + half)
        s = dot(q_ref[rows, :], k_ref[:count, :], 1, 1) * scale
        r = lax.broadcasted_iota(jnp.int32, (half, count), 0) + first
        c = lax.broadcasted_iota(jnp.int32, (half, count), 1)
        s = jnp.where((c <= r) & (c < valid), s, -1e30)
        e = jnp.exp(s - jnp.max(s, axis=1, keepdims=True))
        p = (e / jnp.sum(e, axis=1, keepdims=True)).astype(BF16)
        p_ref[0, rows, :count] = p
        local = dot(p, v_ref[:count, :], 1, 0)
        attn = gate * recalled[rows] + (1.0 - gate) * local
        attn_ref[rows, :] = jnp.where(row_mask(half, valid, first), attn, 0.0).astype(BF16)


def recall_back(lifted, mem, da, gate):
    hd = lifted.shape[1]
    recall = dot(lifted, mem, 1, 1)
    inv = 1.0 / (1.0 + recall[:, hd:hd + 1])
    dnum = da * (gate * inv)
    dden = -jnp.sum(dnum * recall[:, :hd], axis=1, keepdims=True) * inv
    high = dden.astype(BF16).astype(F32)
    lane = lax.broadcasted_iota(jnp.int32, (lifted.shape[0], EXT), 1)
    tail = jnp.where(lane == 0, high, jnp.where(lane == 1, dden - high, 0.0))
    return jnp.concatenate([dnum.astype(BF16), tail.astype(BF16)], axis=1)


def grad_state_kernel(valid_ref, gate_ref, q_ref, mem_ref, da_ref, out_ref):
    seg, hd = q_ref.shape
    gate = gate_ref[pl.program_id(0)]
    live = row_mask(seg, valid_ref[0])
    da = jnp.where(live, da_ref[...].astype(F32), 0.0)
    lifted = lift(q_ref[...].astype(F32)).astype(BF16)
    ext = recall_back(lifted, mem_ref[0], da, gate)
    out = dot(ext, lifted, 0, 0)
    out_ref[0, :hd] = out[:hd].astype(BF16)
    norm = out[hd:hd + 1] + out[hd + 1:hd + 2]
    out_ref[0, hd:] = jnp.broadcast_to(norm, (EXT, hd)).astype(BF16)


def backward_kernel(valid_ref, gate_ref, q_ref, k_ref, v_ref, p_ref, mem_ref, da_ref, dq_ref, dk_ref, dv_ref):
    seg, hd = q_ref.shape
    gate = gate_ref[pl.program_id(0)]
    live = row_mask(seg, valid_ref[0])
    da = jnp.where(live, da_ref[...].astype(F32), 0.0)
    q32 = q_ref[...].astype(F32)
    lifted = lift(q32).astype(BF16)
    ext = recall_back(lifted, mem_ref[0], da, gate)
    dlifted = dot(ext, mem_ref[0], 1, 0)
    do = ((1.0 - gate) * da).astype(BF16)
    p = p_ref[0]
    dv_ref[...] = dot(p, do, 0, 0)
    dp = dot(do, v_ref[...], 1, 1)
    p32 = p.astype(F32)
    weighted = p32 * dp
    ds = (weighted - p32 * jnp.sum(weighted, axis=1, keepdims=True)).astype(BF16)
    scale = hd ** -0.5
    dk_ref[...] = dot(ds, q_ref[...], 0, 0) * scale
    dq = dot(ds, k_ref[...], 1, 0) * scale + dlifted * lift_slope(q32)
    dq_ref[...] = dq.astype(BF16)


def final_kernel(valid_ref, weight_ref, k_ref, v_ref, all_ref, dk_ref, dv_ref, outk_ref, outv_ref):
    seg, hd = k_ref.shape
    live = row_mask(seg, valid_ref[0])
    total = total_state(weight_ref, all_ref)
    row = lax.broadcasted_iota(jnp.int32, total.shape, 0)
    total = jnp.where(row <= hd, total, 0.0).astype(BF16)
    k32 = k_ref[...].astype(F32)
    dlifted = dot(with_ones(v_ref[...]), total, 1, 0)
    slope = jnp.where(live, lift_slope(k32), 0.0)
    outk_ref[...] = (dk_ref[...] + dlifted * slope).astype(BF16)
    lifted = jnp.where(live, lift(k32), 0.0).astype(BF16)
    outv_ref[...] = (dv_ref[...] + dot(lifted, total[:hd], 1, 1)).astype(BF16)


def product_kernel(a_ref, w_ref, out_ref):
    out_ref[0] = dot(a_ref[...], w_ref[0], 1, 0).astype(BF16)


def grad_product_kernel(u_ref, w_ref, out_ref, acc_ref):
    t = pl.program_id(0)
    part = dot(u_ref[0], w_ref[0], 1, 1)

    @pl.when(t == 0)
    def _():
        acc_ref[...] = part

    @pl.when(t > 0)
    def _():
        acc_ref[...] += part

    @pl.when(t == pl.num_programs(0) - 1)
    def _():
        out_ref[...] = acc_ref[...].astype(BF16)


def cost(flops, nbytes):
    return pl.CostEstimate(flops=int(flops), bytes_accessed=int(nbytes), transcendentals=0)


def per_device(q, k, v, upstream, out_weight, gate_logit, document_ids, valid_lengths):
    heads = gate_logit.shape[0]
    seg, width = q.shape
    hd = width // heads
    nseq, nhead = lax.axis_size("seq"), lax.axis_size("head")
    me = lax.axis_index("seq")
    gates = jax.nn.sigmoid(gate_logit)
    valid = lax.dynamic_slice(valid_lengths, (me,), (1,))
    same = document_ids == lax.dynamic_slice(document_ids, (me,), (1,))
    index = jnp.arange(nseq, dtype=jnp.int32)
    earlier = (same & (index < me)).astype(jnp.int32)
    later = (same & (index > me)).astype(jnp.int32)

    col = pl.BlockSpec((seg, hd), lambda h: (0, h))
    state = pl.BlockSpec((1, hd + EXT, hd), lambda h: (h, 0, 0))
    states = pl.BlockSpec((nseq, 1, hd + EXT, hd), lambda h: (0, h, 0, 0))
    square = pl.BlockSpec((1, seg, seg), lambda h: (h, 0, 0))
    state_shape = jax.ShapeDtypeStruct((heads, hd + EXT, hd), BF16)
    big16 = jax.ShapeDtypeStruct((seg, width), BF16)
    big32 = jax.ShapeDtypeStruct((seg, width), F32)
    unit = 2.0 * heads * seg * hd

    kv = pl.pallas_call(
        state_kernel, grid=(heads,), in_specs=[SMEM, col, col], out_specs=state,
        out_shape=state_shape, compiler_params=PARAMS, name="states",
        cost_estimate=cost(unit * hd, 4 * seg * width),
    )(valid, k, v)
    kv_all = lax.all_gather(kv, "seq")
    w_all = lax.all_gather(out_weight, "seq")
    u_all = lax.all_gather(upstream, "head")

    attn, p, mem = pl.pallas_call(
        forward_kernel, grid=(heads,), in_specs=[SMEM, SMEM, SMEM, col, col, col, states],
        out_specs=[col, square, state],
        out_shape=[big16, jax.ShapeDtypeStruct((heads, seg, seg), BF16), state_shape],
        compiler_params=PARAMS, name="forward",
        cost_estimate=cost(unit * (3 * seg + hd), 8 * seg * width + 2 * heads * seg * seg),
    )(valid, earlier, gates, q, k, v, kv_all)

    wcols = out_weight.shape[1]
    per = nseq // nhead
    full = pl.BlockSpec((seg, width), lambda t: (0, 0))
    wspec = pl.BlockSpec((1, width, wcols), lambda t: (t, 0, 0))
    partspec = pl.BlockSpec((1, seg, wcols), lambda t: (t // per, 0, t % per))
    terms = pl.pallas_call(
        product_kernel, grid=(nseq,), in_specs=[full, wspec], out_specs=partspec,
        out_shape=jax.ShapeDtypeStruct((nhead, seg, wcols * per), BF16),
        compiler_params=PARAMS, name="project",
        cost_estimate=cost(2.0 * seg * width * wcols * nseq, 2 * (width + seg) * wcols * nseq),
    )(attn, w_all)
    mixed = lax.psum_scatter(terms, "head", scatter_dimension=0, tiled=False)

    da = pl.pallas_call(
        grad_product_kernel, grid=(nseq,), in_specs=[partspec, wspec], out_specs=full,
        out_shape=big16, scratch_shapes=[pltpu.VMEM((seg, width), F32)],
        compiler_params=PARAMS, name="grad_attn",
        cost_estimate=cost(2.0 * seg * width * wcols * nseq, 2 * (width + seg) * wcols * nseq),
    )(u_all, w_all)
    gm = pl.pallas_call(
        grad_state_kernel, grid=(heads,), in_specs=[SMEM, SMEM, col, state, col],
        out_specs=state, out_shape=state_shape, compiler_params=PARAMS, name="grad_states",
        cost_estimate=cost(unit * hd * 2, 4 * seg * width),
    )(valid, gates, q, mem, da)
    gm_all = lax.all_gather(gm, "seq")
    dq, dk, dv = pl.pallas_call(
        backward_kernel, grid=(heads,),
        in_specs=[SMEM, SMEM, col, col, col, square, state, col], out_specs=[col, col, col],
        out_shape=[big16, big32, big32], compiler_params=PARAMS, name="backward",
        cost_estimate=cost(unit * (4 * seg + 2 * hd), 18 * seg * width + 2 * heads * seg * seg),
    )(valid, gates, q, k, v, p, mem, da)
    gk, gv = pl.pallas_call(
        final_kernel, grid=(heads,), in_specs=[SMEM, SMEM, col, col, states, col, col],
        out_specs=[col, col], out_shape=[big16, big16], compiler_params=PARAMS, name="final",
        cost_estimate=cost(unit * hd * 2, 16 * seg * width),
    )(valid, later, k, v, gm_all, dk, dv)
    return mixed, dq, gk, gv


def solution(mesh):
    spec = P("seq", "head")
    return jax.shard_map(
        per_device,
        mesh=mesh,
        in_specs=(spec, spec, spec, spec, P("head", "seq"), P("head"), P(), P()),
        out_specs=(spec, spec, spec, spec),
        check_vma=False,
    )
```

profile of v0, /device:TPU:7, one launch (start us, length us, event | category | flops | bytes accessed | tf_op | source)
XLA Modules:
  0.0 324.4 jit_solution(601934180143908068)
XLA Ops:
  7.2 0.0 copy-start.21
  7.2 0.0 copy-start.22
  7.2 0.0 all-gather.9.cloned.1.call-start
  7.2 1.3 dynamic_slice.6.valid_ref
  8.5 0.0 copy-start
  8.5 1.2 copy-done
  9.8 0.0 copy-start.2
  9.8 1.2 copy-done.2
  11.0 0.0 copy-start.1
  11.0 0.0 copy-start.3
  11.0 0.0 copy-start.10
  11.0 4.9 %states.1 = bf16[8,144,128]{2,1,0:T(8,128)(2,1)} custom-call(s32[1]{0:T(128)} %dynamic_slice.6.valid_ref, bf16[512,1024]{1,0:T(8,128)(2,1)S(1)} %copy-done, bf16[512,1024]{1,0:T(8,128)(2,1)S(1)} %copy-done.2), custom_call_target="tpu_custom_call" | custom-call | flops 134217728 | bytes 2097152 | tf_op jit(solution)/shard_map/states/pallas_call | solution.py:186
  15.9 0.0 all-gather.9.cloned.1.call-update
  16.0 0.0 all-gather.13.cloned.1.call-start
  16.0 0.7 all-gather.13.cloned.1.call-update
  16.7 0.0 all-gather.11.cloned.1.call-start
  16.8 0.7 all-gather.11.cloned.1.call-update
  17.4 0.0 all-gather.15.cloned.1.call-start
  17.5 0.0 copy-done.21
  17.5 0.6 dynamic_slice.7
  18.1 0.0 copy-done.22
  18.1 0.7 and_convert_fusion
  18.8 27.1 %all-gather.9.cloned.1.call-done = bf16[64,144,128]{2,1,0:T(8,128)(2,1)} async-done(((bf16[8,144,128]{2,1,0:T(8,128)(2,1)}), bf16[64,144,128]{2,1,0:T(8,128)(2,1)}) %all-gather.9.cloned.1.call-update) | async-done | bytes 2359312 | tf_op jit(solution)/shard_map/all_gather | solution.py:191
  45.8 0.0 copy-done.1
  45.8 0.0 copy-done.3
  45.8 0.0 copy-done.10
  45.8 0.0 copy-start.16
  45.8 1.7 copy-done.16
  47.5 10.5 %forward.1 = (bf16[512,1024]{1,0:T(8,128)(2,1)S(1)}, bf16[8,512,512]{2,1,0:T(8,128)(2,1)S(1)}, bf16[8,144,128]{2,1,0:T(8,128)(2,1)S(1)}) custom-call(s32[1]{0:T(128)} %dynamic_slice.6.valid_ref, s32[8]{0:T(128)S(1)} %get-tuple-element.21.weight_ref, f32[8]{0:T(128)S(1)} %add_divide_fusion.gate_ref, bf16[512,1024]{1,0:T(8,128)(2,1)S(1)} %copy-done.10, ...), custom_call_target="tpu_custom_call" | custom-call | flops 1744830464 | bytes 8388608 | tf_op jit(solution)/shard_map/forward/pallas_call | solution.py:195
  58.0 0.0 copy-start.17
  58.0 2.0 copy-done.17
  60.0 0.0 copy-start.19
  60.0 1.0 copy-done.19
  61.0 67.7 %all-gather.13.cloned.1.call-done = bf16[2048,1024]{1,0:T(8,128)(2,1)} async-done(((bf16[512,1024]{1,0:T(8,128)(2,1)}), bf16[2048,1024]{1,0:T(8,128)(2,1)}) %all-gather.13.cloned.1.call-update) | async-done | bytes 4194320 | tf_op jit(solution)/shard_map/all_gather | solution.py:193
  128.7 54.3 %all-gather.11.cloned.1.call-done = bf16[8192,512]{1,0:T(8,128)(2,1)} async-done(((bf16[1024,512]{1,0:T(8,128)(2,1)}), bf16[8192,512]{1,0:T(8,128)(2,1)}) %all-gather.11.cloned.1.call-update) | async-done | bytes 8388624 | tf_op jit(solution)/shard_map/all_gather | solution.py:192
  183.0 0.0 copy-start.13
  183.0 3.4 %copy-done.13 = bf16[8192,512]{1,0:T(8,128)(2,1)S(1)} copy-done((bf16[8192,512]{1,0:T(8,128)(2,1)S(1)}, bf16[8192,512]{1,0:T(8,128)(2,1)}, u32[]{:S(2)}) %copy-start.13) | copy-done | bytes 8388632
  186.4 2.2 copy-done.15
  188.6 8.0 %grad_attn.1.da_ref = bf16[512,1024]{1,0:T(8,128)(2,1)S(1)} custom-call(bf16[4,512,1024]{2,1,0:T(8,128)(2,1)S(1)} %bitcast.9, bf16[8,1024,512]{2,1,0:T(8,128)(2,1)S(1)} %bitcast.7), custom_call_target="tpu_custom_call" | custom-call | flops 4294967296 | bytes 12582912 | tf_op jit(solution)/shard_map/grad_attn/pallas_call | solution.py:216
  196.6 11.0 %grad_states.1 = bf16[8,144,128]{2,1,0:T(8,128)(2,1)} custom-call(s32[1]{0:T(128)} %dynamic_slice.6.valid_ref, f32[8]{0:T(128)S(1)} %add_divide_fusion.gate_ref, bf16[512,1024]{1,0:T(8,128)(2,1)S(1)} %copy-done.10, bf16[8,144,128]{2,1,0:T(8,128)(2,1)S(1)} %get-tuple-element.14.mem_ref, bf16[512,1024]{1,0:T(8,128)(2,1)S(1)} %grad_attn.1.da_ref), custom_call_target="tpu_custom_call" | custom-call | flops 268435456 | bytes 2097152 | tf_op jit(solution)/shard_map/grad_states/pallas_call | solution.py:222
  207.6 0.0 copy-start.11
  207.6 1.0 copy-done.11
  208.6 0.0 all-gather.15.cloned.1.call-update
  208.6 0.0 reduce-scatter.2.cloned.1.call-start
  208.7 0.0 copy-start.14
  208.7 3.4 %copy-done.14 = bf16[8192,512]{1,0:T(8,128)(2,1)S(1)} copy-done((bf16[8192,512]{1,0:T(8,128)(2,1)S(1)}, bf16[8192,512]{1,0:T(8,128)(2,1)}, u32[]{:S(2)}) %copy-start.14) | copy-done | bytes 8388632
  212.1 0.0 copy-start.20
  212.1 1.2 copy-done.20
  213.3 6.1 %project.1 = bf16[4,512,1024]{2,1,0:T(8,128)(2,1)S(1)} custom-call(bf16[512,1024]{1,0:T(8,128)(2,1)S(1)} %copy-done.20, bf16[8,1024,512]{2,1,0:T(8,128)(2,1)S(1)} %bitcast.8), custom_call_target="tpu_custom_call" | custom-call | flops 4294967296 | bytes 12582912 | tf_op jit(solution)/shard_map/project/pallas_call | solution.py:208
  219.4 0.0 copy-start.4
  219.5 2.0 copy-done.4
  221.4 0.0 reduce-scatter.2.cloned.1.call-update
  221.5 0.0 copy-start.12
  221.5 1.2 copy-done.12
  222.7 0.0 copy-start.18
  222.7 2.2 copy-done.18
  224.9 16.8 %backward.1 = (bf16[512,1024]{1,0:T(8,128)(2,1)}, f32[512,1024]{1,0:T(8,128)S(1)}, f32[512,1024]{1,0:T(8,128)S(1)}) custom-call(s32[1]{0:T(128)} %dynamic_slice.6.valid_ref, f32[8]{0:T(128)S(1)} %add_divide_fusion.gate_ref, bf16[512,1024]{1,0:T(8,128)(2,1)S(1)} %copy-done.10, bf16[512,1024]{1,0:T(8,128)(2,1)S(1)} %copy-done.1, ...), custom_call_target="tpu_custom_call" | custom-call | flops 2415919104 | bytes 13631488 | tf_op jit(solution)/shard_map/backward/pallas_call | solution.py:228
  241.7 1.4 copy-done.6
  243.1 1.4 copy-done.8
  244.5 1.7 copy-done.5
  246.2 1.7 copy-done.7
  247.8 1.8 copy-done.9
  249.7 6.3 %final.1 = (bf16[512,1024]{1,0:T(8,128)(2,1)}, bf16[512,1024]{1,0:T(8,128)(2,1)}) custom-call(s32[1]{0:T(128)} %dynamic_slice.6.valid_ref, s32[8]{0:T(128)S(1)} %get-tuple-element.20.weight_ref, bf16[512,1024]{1,0:T(8,128)(2,1)S(1)} %copy-done.1, bf16[512,1024]{1,0:T(8,128)(2,1)S(1)} %copy-done.3, bf16[8,8,144,128]{3,2,1,0:T(8,128)(2,1)S(1)} %bitcast.6, ...), custom_call_target="tpu_custom_call" | custom-call | flops 268435456 | bytes 8388608 | tf_op jit(solution)/shard_map/final/pallas_call | solution.py:234
  256.0 61.9 %reduce-scatter.2.cloned.1.call-done = bf16[1,512,1024]{2,1,0:T(8,128)(2,1)} async-done(((bf16[4,512,1024]{2,1,0:T(8,128)(2,1)}), bf16[1,512,1024]{2,1,0:T(8,128)(2,1)}) %reduce-scatter.2.cloned.1.call-update) | async-done | bytes 1048592 | tf_op jit(solution)/shard_map/reduce_scatter | solution.py:214
  (8 shorter events, 0.0 us)
Async XLA Ops:
  7.2 10.3 %copy-start.21 = (s32[8]{0:T(128)S(1)}, s32[8]{0:T(128)}, u32[]{:S(2)}) copy-start(s32[8]{0:T(128)} %param.14) | copy-start | bytes 100
  7.2 10.9 %copy-start.22 = (f32[8]{0:T(128)S(1)}, f32[8]{0:T(128)}, u32[]{:S(2)}) copy-start(f32[8]{0:T(128)} %param.13) | copy-start | bytes 100
  7.2 38.6 %all-gather.9.cloned.1.call-start = ((), (), s32[]{:S(2)}) async-start(), calls=%async_computation.2 | async-start | bytes 2654208 | tf_op jit(solution)/shard_map/all_gather | solution.py:191
  8.5 1.2 copy-start
  9.8 1.2 copy-start.2
  11.0 34.8 %copy-start.1 = (bf16[512,1024]{1,0:T(8,128)(2,1)S(1)}, bf16[512,1024]{1,0:T(8,128)(2,1)}, u32[]{:S(2)}) copy-start(bf16[512,1024]{1,0:T(8,128)(2,1)} %k_ref.7) | copy-start | bytes 3145732
  11.0 34.8 %copy-start.3 = (bf16[512,1024]{1,0:T(8,128)(2,1)S(1)}, bf16[512,1024]{1,0:T(8,128)(2,1)}, u32[]{:S(2)}) copy-start(bf16[512,1024]{1,0:T(8,128)(2,1)} %v_ref.7) | copy-start | bytes 3145732
  11.0 34.8 %copy-start.10 = (bf16[512,1024]{1,0:T(8,128)(2,1)S(1)}, bf16[512,1024]{1,0:T(8,128)(2,1)}, u32[]{:S(2)}) copy-start(bf16[512,1024]{1,0:T(8,128)(2,1)} %q_ref.5) | copy-start | bytes 3145732
  16.0 112.7 %all-gather.13.cloned.1.call-start = ((), (), s32[]{:S(2)}) async-start(), calls=%async_computation.4 | async-start | bytes 5242880 | tf_op jit(solution)/shard_map/all_gather | solution.py:193
  16.7 166.3 %all-gather.11.cloned.1.call-start = ((), (), s32[]{:S(2)}) async-start(), calls=%async_computation.3 | async-start | bytes 9437184 | tf_op jit(solution)/shard_map/all_gather | solution.py:192
  17.4 227.1 %all-gather.15.cloned.1.call-start = ((), (), s32[]{:S(2)}) async-start(), calls=%async_computation.5 | async-start | bytes 2654208 | tf_op jit(solution)/shard_map/all_gather | solution.py:227
  45.8 1.7 copy-start.16
  58.0 2.0 copy-start.17
  60.0 1.0 copy-start.19
  183.0 3.4 %copy-start.13 = (bf16[8192,512]{1,0:T(8,128)(2,1)S(1)}, bf16[8192,512]{1,0:T(8,128)(2,1)}, u32[]{:S(2)}) copy-start(bf16[8192,512]{1,0:T(8,128)(2,1)} %all-gather.11.cloned.1.call-done) | copy-start | bytes 25165828
  186.4 2.2 copy-start.15
  207.6 1.0 copy-start.11
  208.6 109.2 %reduce-scatter.2.cloned.1.call-start = ((), (), s32[]{:S(2)}) async-start(), calls=%async_computation.1 | async-start | bytes 5242880 | tf_op jit(solution)/shard_map/reduce_scatter | solution.py:214
  208.7 3.4 %copy-start.14 = (bf16[8192,512]{1,0:T(8,128)(2,1)S(1)}, bf16[8192,512]{1,0:T(8,128)(2,1)}, u32[]{:S(2)}) copy-start(bf16[8192,512]{1,0:T(8,128)(2,1)} %all-gather.11.cloned.1.call-done) | copy-start | bytes 25165828
  212.1 1.2 copy-start.20
  219.4 2.0 copy-start.4
  221.5 1.2 copy-start.12
  222.7 2.2 copy-start.18
  241.7 1.4 copy-start.6
  243.1 1.4 copy-start.8
  244.5 1.7 copy-start.5
  246.2 1.7 copy-start.7
  247.8 1.8 copy-start.9
Sparse Core Ops, SparseCore 0:
  16.1 29.6 all-gather.8
  47.4 81.2 all-gather.12
  130.6 52.3 all-gather.10
  208.8 29.0 all-gather.14
  240.5 77.2 reduce-scatter.1
where the time goes:
time: 326 us; the launch traced here: 324 us
  waiting for transfers between devices  212 us (65%)
  Pallas kernels  63.8 us (20%)
  local copies, waits for them, and re-layouts  33.4 us (10%)
  between operations  13.9 us (4%)
    all_gather x1, waiting for transfers between devices, per_device(): u_all = lax.all_gather(upstream, 'head')  67.7 us
    reduce_scatter x1, waiting for transfers between devices, per_device(): mixed = lax.psum_scatter(terms, 'head', scatter_dimension=0, tiled=False)  61.9 us
    all_gather x1, waiting for transfers between devices, per_device(): w_all = lax.all_gather(out_weight, 'seq')  54.3 us
    unnamed x46, local copies, waits for them, and re-layouts  31.6 us
    all_gather x1, waiting for transfers between devices, per_device(): kv_all = lax.all_gather(kv, 'seq')  27.1 us
    pallas_call x1, Pallas kernels, per_device(): pl.pallas_call(backward_kernel, grid=(heads,), in_specs=[SMEM, SMEM, col,...  16.8 us
    pallas_call x1, Pallas kernels, per_device(): pl.pallas_call(grad_state_kernel, grid=(heads,), in_specs=[SMEM, SMEM, co...  11 us
    pallas_call x1, Pallas kernels, per_device(): pl.pallas_call(forward_kernel, grid=(heads,), in_specs=[SMEM, SMEM, SMEM,...  10.5 us
  transfers between devices with their start and end apart: 5, of which 4 were waited for; matrix products, arithmetic and copies ran while one was open for 0% of the time, Pallas kernels for 12%

commit v1 on v0

v1 whole, which is shorter than its diff:
```python
import functools

import jax
import jax.numpy as jnp
from jax import lax
from jax.experimental import pallas as pl
from jax.experimental.pallas import tpu as pltpu
from jax.sharding import PartitionSpec as P

F32 = jnp.float32
BF16 = jnp.bfloat16
EXT = 16
MESH = pl.DeviceIdType.MESH


def lift(x):
    return jnp.where(x > 0, x + 1.0, jnp.exp(jnp.minimum(x, 0.0)))


def lift_slope(x):
    return jnp.where(x > 0, 1.0, jnp.exp(jnp.minimum(x, 0.0)))


def dot(a, b, ca, cb):
    return lax.dot_general(a, b, (((ca,), (cb,)), ((), ())), preferred_element_type=F32)


def row_mask(rows, valid, first=0):
    return lax.broadcasted_iota(jnp.int32, (rows, 1), 0) + first < valid


def with_ones(v):
    return jnp.concatenate([v, jnp.ones((v.shape[0], EXT), v.dtype)], axis=1)


def kernel(
    nseq, nhead, heads,
    valid_ref, doc_ref, gate_ref, q_ref, k_ref, v_ref, u_ref, w_ref,
    mixed_ref, dq_ref, gk_ref, gv_ref,
    wall, uall, terms, parts, probs, acc, lifted_ref, recalled_ref, ginv_ref,
    dk_ref, dv_ref, attn_ref, da_ref, mem_ref, kv_own, kv_in, gm_own, gm_in,
    w_send, w_pass, w_recv, u_send, u_recv, kv_send, kv_recv, gm_send, gm_recv,
    p_send, p_recv, own_sem,
):
    seg, width = q_ref.shape
    hd = width // heads
    half = seg // 2
    span = nseq // 2
    chips = nseq // 2
    per = nseq // nhead
    wcols = w_ref.shape[1]
    scale = hd ** -0.5
    me = lax.axis_index("seq")
    z = lax.axis_index("head")
    chip, core = me // 2, me % 2
    partner = chip * 2 + 1 - core
    has_left, has_right = z > 0, z < nhead - 1

    barrier = pltpu.get_barrier_semaphore()
    for d in range(1, nseq):
        pl.semaphore_signal(
            barrier, inc=1, device_id=((me + d) % nseq, z), device_id_type=MESH
        )

    for d in range(1, nhead):
        pl.semaphore_signal(
            barrier, inc=1, device_id=(me, (z + d) % nhead), device_id_type=MESH
        )
    pl.semaphore_wait(barrier, nseq + nhead - 2)

    def remote(src, dst, send, recv, seq, head):
        return pltpu.make_async_remote_copy(
            src_ref=src, dst_ref=dst, send_sem=send, recv_sem=recv,
            device_id=(seq, head), device_id_type=MESH,
        )

    def u_copy(way, hop):
        block = z - hop if way == 0 else z + hop
        to = z + 1 if way == 0 else z - 1
        src = u_ref if hop == 0 else uall.at[block]
        return remote(src, uall.at[block], u_send.at[way, hop], u_recv.at[block], me, to)

    def u_sends(way, hop):
        if way == 0:
            return has_right & (z >= hop)
        return has_left & (z + hop <= nhead - 1)

    def u_wait(block):
        remote(u_ref, uall.at[block], u_send.at[0, 0], u_recv.at[block], me, z).wait_recv()

    def u_arrived(hop):
        for way in range(2):
            block = z - hop if way == 0 else z + hop
            there = (z >= hop) if way == 0 else (z + hop <= nhead - 1)

            @pl.when(there)
            def _():
                u_wait(block)

            if hop < nhead - 1:

                @pl.when(u_sends(way, hop))
                def _():
                    u_copy(way, hop).start()

    for way in range(2):

        @pl.when(u_sends(way, 0))
        def _():
            u_copy(way, 0).start()

    def w_to_partner(delta):
        block = ((chip - delta + chips) % chips) * 2 + core
        src = w_ref if delta == 0 else wall.at[block]
        return remote(src, wall.at[block], w_pass.at[delta], w_recv.at[block], partner, z)

    def w_to_chip(delta):
        to = ((chip + delta) % chips) * 2 + core
        return remote(w_ref, wall.at[me], w_send.at[delta], w_recv.at[me], to, z)

    def w_wait(block):
        remote(w_ref, wall.at[block], w_pass.at[0], w_recv.at[block], partner, z).wait_recv()

    w_to_partner(0).start()
    own_w = pltpu.make_async_copy(w_ref, wall.at[me], own_sem.at[0])
    own_w.start()
    own_u = pltpu.make_async_copy(u_ref, uall.at[z], own_sem.at[1])
    own_u.start()

    valid = valid_ref[me]
    live = row_mask(seg, valid)

    def lanes(h):
        return pl.ds(pl.multiple_of(h * hd, hd), hd)

    def gate_of(h):
        return 1.0 / (1.0 + jnp.exp(jnp.full((1, hd), -gate_ref[h], F32)))

    def over_heads(body):
        def step(h, carry):
            body(h)
            return carry

        lax.fori_loop(0, heads, step, 0)

    @over_heads
    def _(h):
        lifted = jnp.where(live, lift(k_ref[:, lanes(h)].astype(F32)), 0.0).astype(BF16)
        kv_own[h] = dot(with_ones(v_ref[:, lanes(h)]), lifted, 0, 0).astype(BF16)

    def kv_copy(d):
        return remote(
            kv_own, kv_in.at[d - 1], kv_send.at[d - 1], kv_recv.at[d - 1], (me + d) % nseq, z
        )

    def gm_copy(d):
        return remote(
            gm_own, gm_in.at[d - 1], gm_send.at[d - 1], gm_recv.at[d - 1],
            (me - d + nseq) % nseq, z,
        )

    for d in range(1, span):
        kv_copy(d).start()
    for delta in range(1, chips):
        w_to_chip(delta).start()

    @over_heads
    def _(h):
        keep = 1.0 - gate_of(h)
        probs[h, :half, half:] = jnp.zeros((half, seg - half), BF16)
        for first, count in ((0, half), (half, seg)):
            rows = slice(first, first + half)
            s = dot(q_ref[rows, lanes(h)], k_ref[:count, lanes(h)], 1, 1) * scale
            r = lax.broadcasted_iota(jnp.int32, (half, count), 0) + first
            c = lax.broadcasted_iota(jnp.int32, (half, count), 1)
            s = jnp.where((c <= r) & (c < valid), s, -1e30)
            e = jnp.exp(s - jnp.max(s, axis=1, keepdims=True))
            p = (e * (1.0 / jnp.sum(e, axis=1, keepdims=True))).astype(BF16)
            probs[h, rows, :count] = p
            acc[rows, lanes(h)] = keep * dot(p, v_ref[:count, lanes(h)], 1, 0)

    def weight_of(d, earlier):
        other = me - d if earlier else me + d
        inside = (other >= 0) if earlier else (other < nseq)
        index = (other + nseq) % nseq
        return (inside & (doc_ref[index] == doc_ref[me])).astype(F32)

    for d in range(1, span):
        kv_copy(d).wait_recv()

    def total_state(slots, earlier, h):
        total = jnp.zeros((hd + EXT, hd), F32)
        for d in range(1, span):
            total = total + weight_of(d, earlier) * slots[d - 1, h].astype(F32)
        return total

    @over_heads
    def _(h):
        gate = gate_of(h)
        mem = total_state(kv_in, True, h).astype(BF16)
        mem_ref[h] = mem
        lifted = lift(q_ref[:, lanes(h)].astype(F32)).astype(BF16)
        lifted_ref[:, lanes(h)] = lifted
        recall = dot(lifted, mem, 1, 1)
        inv = 1.0 / (1.0 + recall[:, hd:hd + 1])
        recalled = recall[:, :hd] * inv
        recalled_ref[:, lanes(h)] = recalled.astype(BF16)
        ginv_ref[:, lanes(h)] = jnp.where(live, gate * inv, 0.0)
        attn = gate * recalled + acc[:, lanes(h)]
        attn_ref[:, lanes(h)] = jnp.where(live, attn, 0.0).astype(BF16)

    def p_copy(block):
        owner, sub = block // per, block % per
        return remote(
            terms.at[block], parts.at[z, sub], p_send.at[block], p_recv.at[z, sub], me, owner
        )

    def project(block):
        terms[block] = dot(attn_ref[...], wall[block], 1, 0).astype(BF16)

        @pl.when(block // per != z)
        def _():
            p_copy(block).start()

    own_w.wait()
    project(me)
    w_wait(partner)
    project(partner)
    for delta in range(1, chips):
        base = ((chip - delta + chips) % chips) * 2
        w_wait(base + core)
        w_to_partner(delta).start()
        if delta < nhead - 1:
            u_arrived(delta)
        project(base + core)
        w_wait(base + 1 - core)
        project(base + 1 - core)

    def grad_product(block):
        for sub in range(per):
            acc[...] += dot(
                uall[block, :, sub * wcols:(sub + 1) * wcols], wall[block * per + sub], 1, 1
            )

    own_u.wait()
    acc[...] = jnp.zeros_like(acc)
    grad_product(z)
    for hop in range(1, nhead):
        if hop >= min(chips, nhead - 1):
            u_arrived(hop)
        for way in range(2):
            there = (z >= hop) if way == 0 else (z + hop <= nhead - 1)

            @pl.when(there)
            def _():
                grad_product(z - hop if way == 0 else z + hop)

    def rounded_grad(h):
        da = acc[:, lanes(h)].astype(BF16)
        return jnp.where(live, da.astype(F32), 0.0)

    def recall_back(h, da):
        dnum = da * ginv_ref[:, lanes(h)]
        dden = -jnp.sum(dnum * recalled_ref[:, lanes(h)].astype(F32), axis=1, keepdims=True)
        high = dden.astype(BF16).astype(F32)
        lane = lax.broadcasted_iota(jnp.int32, (seg, EXT), 1)
        tail = jnp.where(lane == 0, high, jnp.where(lane == 1, dden - high, 0.0))
        return jnp.concatenate([dnum.astype(BF16), tail.astype(BF16)], axis=1)

    @over_heads
    def _(h):
        ext = recall_back(h, rounded_grad(h))
        out = dot(ext, lifted_ref[:, lanes(h)], 0, 0)
        gm_own[h, :hd] = out[:hd].astype(BF16)
        norm = out[hd:hd + 1] + out[hd + 1:hd + 2]
        row = lax.broadcasted_iota(jnp.int32, (EXT, hd), 0)
        gm_own[h, hd:] = jnp.where(row == 0, norm, 0.0).astype(BF16)

    for d in range(1, span):
        gm_copy(d).start()

    @over_heads
    def _(h):
        da = rounded_grad(h)
        ext = recall_back(h, da)
        dlifted = dot(ext, mem_ref[h], 1, 0)
        do = ((1.0 - gate_of(h)) * da).astype(BF16)
        p = probs[h]
        dv_ref[:, lanes(h)] = dot(p, do, 0, 0)
        dp = dot(do, v_ref[:, lanes(h)], 1, 1)
        p32 = p.astype(F32)
        weighted = p32 * dp
        ds = (weighted - p32 * jnp.sum(weighted, axis=1, keepdims=True)).astype(BF16)
        dk_ref[:, lanes(h)] = dot(ds, q_ref[:, lanes(h)], 0, 0) * scale
        dq = dot(ds, k_ref[:, lanes(h)], 1, 0) * scale
        dq_ref[:, lanes(h)] = (
            dq + dlifted * lift_slope(q_ref[:, lanes(h)].astype(F32))
        ).astype(BF16)

    for d in range(1, span):
        gm_copy(d).wait_recv()

    @over_heads
    def _(h):
        total = total_state(gm_in, False, h).astype(BF16)
        k32 = k_ref[:, lanes(h)].astype(F32)
        dlifted = dot(with_ones(v_ref[:, lanes(h)]), total, 1, 0)
        slope = jnp.where(live, lift_slope(k32), 0.0)
        gk_ref[:, lanes(h)] = (dk_ref[:, lanes(h)] + dlifted * slope).astype(BF16)
        lifted = jnp.where(live, lift(k32), 0.0).astype(BF16)
        gv_ref[:, lanes(h)] = (
            dv_ref[:, lanes(h)] + dot(lifted, total[:hd], 1, 1)
        ).astype(BF16)

    for step in range(1, nhead):
        other = (z + step) % nhead
        for sub in range(per):
            remote(
                terms.at[sub], parts.at[other, sub], p_send.at[sub], p_recv.at[other, sub], me,
                other,
            ).wait_recv()
    for sub in range(per):
        total = terms[z * per + sub].astype(F32)
        for step in range(1, nhead):
            total = total + parts[(z + step) % nhead, sub].astype(F32)
        mixed_ref[:, sub * wcols:(sub + 1) * wcols] = total.astype(BF16)

    for step in range(1, nhead):
        for sub in range(per):
            p_copy(((z + step) % nhead) * per + sub).wait_send()
    for d in range(1, span):
        kv_copy(d).wait_send()
        gm_copy(d).wait_send()
    for delta in range(chips):
        w_to_partner(delta).wait_send()
        if delta > 0:
            w_to_chip(delta).wait_send()
    for way in range(2):
        for hop in range(nhead - 1):

            @pl.when(u_sends(way, hop))
            def _():
                u_copy(way, hop).wait_send()


def per_device(q, k, v, upstream, out_weight, gate_logit, document_ids, valid_lengths):
    heads = gate_logit.shape[0]
    seg, width = q.shape
    hd = width // heads
    nseq, nhead = lax.axis_size("seq"), lax.axis_size("head")
    wcols = out_weight.shape[1]
    per = nseq // nhead
    span = nseq // 2
    state = (heads, hd + EXT, hd)
    dma = pltpu.SemaphoreType.DMA
    smem = pl.BlockSpec(memory_space=pltpu.SMEM)
    vmem = pl.BlockSpec(memory_space=pltpu.VMEM)
    return pl.pallas_call(
        functools.partial(kernel, nseq, nhead, heads),
        out_shape=[jax.ShapeDtypeStruct((seg, width), BF16)] * 4,
        in_specs=[smem] * 3 + [vmem] * 5,
        out_specs=[vmem] * 4,
        scratch_shapes=[
            pltpu.VMEM((nseq, width, wcols), BF16),
            pltpu.VMEM((nhead, seg, wcols * per), BF16),
            pltpu.VMEM((nseq, seg, wcols), BF16),
            pltpu.VMEM((nhead, per, seg, wcols), BF16),
            pltpu.VMEM((heads, seg, seg), BF16),
            pltpu.VMEM((seg, width), F32),
            pltpu.VMEM((seg, width), BF16),
            pltpu.VMEM((seg, width), BF16),
            pltpu.VMEM((seg, width), F32),
            pltpu.VMEM((seg, width), F32),
            pltpu.VMEM((seg, width), F32),
            pltpu.VMEM((seg, width), BF16),
            pltpu.VMEM((seg, width), BF16),
            pltpu.VMEM(state, BF16),
            pltpu.VMEM(state, BF16),
            pltpu.VMEM((span - 1,) + state, BF16),
            pltpu.VMEM(state, BF16),
            pltpu.VMEM((span - 1,) + state, BF16),
            dma((span,)), dma((span,)), dma((nseq,)),
            dma((2, nhead)), dma((nhead,)),
            dma((span - 1,)), dma((span - 1,)), dma((span - 1,)), dma((span - 1,)),
            dma((nseq,)), dma((nhead, per)), dma((2,)),
        ],
        compiler_params=pltpu.CompilerParams(
            collective_id=0, has_side_effects=True, vmem_limit_bytes=60 * 1024 * 1024
        ),
        cost_estimate=pl.CostEstimate(
            flops=4 * seg * width * wcols * nseq, bytes_accessed=18 * seg * width,
            transcendentals=0,
        ),
        name="layer",
    )(valid_lengths, document_ids, gate_logit, q, k, v, upstream, out_weight)


def solution(mesh):
    spec = P("seq", "head")
    return jax.shard_map(
        per_device,
        mesh=mesh,
        in_specs=(spec, spec, spec, spec, P("head", "seq"), P("head"), P(), P()),
        out_specs=(spec, spec, spec, spec),
        check_vma=False,
    )
```

time: 326 us -> 222 us (0.68)
  waiting for transfers between devices: 212 us -> 0 us
  Pallas kernels: 63.8 us -> 215 us
  local copies, waits for them, and re-layouts: 33.4 us -> 6.53 us
  between operations: 13.9 us -> 0.65 us
    pallas_call x7 -> x1, Pallas kernels: 63.8 us -> 215 us  [per_device(): pl.pallas_call(functools.partial(kernel, nseq, nhead, heads), out_shape=[...]
    all_gather x4 -> x0, waiting for transfers between devices: 149 us -> none  [the longest x1 67.7 us: per_device(): u_all = lax.all_gather(upstream, 'head')]
    reduce_scatter x1 -> x0, waiting for transfers between devices: 61.9 us -> none  [per_device(): mixed = lax.psum_scatter(terms, 'head', scatter_dimension=0, tiled=False)]
    unnamed x46 -> x10, local copies, waits for them, and re-layouts: 31.6 us -> 6.53 us
  transfers between devices with their start and end apart: 5 -> 0, of which waited for: 4 -> 0; matrix products, arithmetic and copies ran while one was open for 0% -> 0% of each run, Pallas kernels for 12% -> 0%
where the time goes in v1:
time: 222 us
  Pallas kernels  215 us (97%)
  local copies, waits for them, and re-layouts  6.53 us (3%)
    pallas_call x1, Pallas kernels, per_device(): pl.pallas_call(functools.partial(kernel, nseq, nhead, heads), out_shape=[...  215 us
    unnamed x10, local copies, waits for them, and re-layouts  6.53 us

profile of v1, /device:TPU:7, one launch (start us, length us, event | category | flops | bytes accessed | tf_op | source)
XLA Modules:
  0.0 221.9 jit_solution(5607661453546880786)
XLA Ops:
  0.6 214.7 %layer.1 = (bf16[512,1024]{1,0:T(8,128)(2,1)}, bf16[512,1024]{1,0:T(8,128)(2,1)}, bf16[512,1024]{1,0:T(8,128)(2,1)}, bf16[512,1024]{1,0:T(8,128)(2,1)}) custom-call(s32[8]{0:T(128)} %valid_ref.1, s32[8]{0:T(128)} %doc_ref.1, f32[8]{0:T(128)} %gate_ref.1, bf16[512,1024]{1,0:T(8,128)(2,1)} %q_ref.1, bf16[512,1024]{1,0:T(8,128)(2,1)} %k_ref.1, ...), custom_call_target="tpu_custom_call" | custom-call | flops 8589934592 | bytes 9437184 | tf_op jit(solution)/shard_map/layer/pallas_call | solution.py:358
  215.4 0.0 copy-start.2
  215.4 2.4 %copy.16 = bf16[512,1024]{1,0:T(8,128)(2,1)} copy(bf16[512,1024]{1,0:T(8,128)(2,1)} %get-tuple-element.8) | data formatting | bytes 2097152
  217.7 0.0 copy-done.2
  217.7 0.0 copy-start.1
  217.7 1.0 copy.17
  218.7 0.6 copy-done.1
  219.3 0.0 copy-start
  219.3 1.0 copy.18
  220.3 0.6 copy-done
  220.9 1.0 copy.19
Async XLA Ops:
  215.4 2.4 %copy-start.2 = (bf16[512,1024]{1,0:T(8,128)(2,1)S(1)}, bf16[512,1024]{1,0:T(8,128)(2,1)}, u32[]{:S(2)}) copy-start(bf16[512,1024]{1,0:T(8,128)(2,1)} %get-tuple-element.9) | copy-start | bytes 3145732
  217.7 1.6 copy-start.1
  219.3 1.6 copy-start

commit v2 on v1

--- a/solution.py
+++ b/solution.py
@@ -10,6 +10,7 @@
 F32 = jnp.float32
 BF16 = jnp.bfloat16
 EXT = 16
+LAG = 2
 MESH = pl.DeviceIdType.MESH
 
 
@@ -37,10 +38,10 @@
     nseq, nhead, heads,
     valid_ref, doc_ref, gate_ref, q_ref, k_ref, v_ref, u_ref, w_ref,
     mixed_ref, dq_ref, gk_ref, gv_ref,
-    wall, uall, terms, parts, probs, acc, lifted_ref, recalled_ref, ginv_ref,
+    wall, uall, right_ref, left_ref, probs, acc, lifted_ref, recalled_ref, ginv_ref,
     dk_ref, dv_ref, attn_ref, da_ref, mem_ref, kv_own, kv_in, gm_own, gm_in,
     w_send, w_pass, w_recv, u_send, u_recv, kv_send, kv_recv, gm_send, gm_recv,
-    p_send, p_recv, own_sem,
+    hop_send, hop_recv, own_sem,
 ):
     seg, width = q_ref.shape
     hd = width // heads
@@ -160,7 +161,11 @@
         )
 
     for d in range(1, span):
-        kv_copy(d).start()
+
+        @pl.when(me + d < nseq)
+        def _():
+            kv_copy(d).start()
+
     for delta in range(1, chips):
         w_to_chip(delta).start()
 
@@ -186,7 +191,14 @@
         return (inside & (doc_ref[index] == doc_ref[me])).astype(F32)
 
     for d in range(1, span):
-        kv_copy(d).wait_recv()
+
+        @pl.when(me >= d)
+        def _():
+            kv_copy(d).wait_recv()
+
+        @pl.when(me < d)
+        def _():
+            kv_in[d - 1] = jnp.zeros(kv_in.shape[1:], BF16)
 
     def total_state(slots, earlier, h):
         total = jnp.zeros((hd + EXT, hd), F32)
@@ -209,32 +221,65 @@
         attn = gate * recalled + acc[:, lanes(h)]
         attn_ref[:, lanes(h)] = jnp.where(live, attn, 0.0).astype(BF16)
 
-    def p_copy(block):
-        owner, sub = block // per, block % per
+    def block_at(i):
+        delta, kind = i // 2, i % 2
+        return ((chip - delta + chips) % chips) * 2 + (core + kind) % 2
+
+    def hop_copy(way, block):
+        slots = right_ref if way == 0 else left_ref
+        to = z + 1 if way == 0 else z - 1
         return remote(
-            terms.at[block], parts.at[z, sub], p_send.at[block], p_recv.at[z, sub], me, owner
+            slots.at[block], slots.at[block], hop_send.at[way, block], hop_recv.at[way, block],
+            me, to,
         )
 
     def project(block):
-        terms[block] = dot(attn_ref[...], wall[block], 1, 0).astype(BF16)
-
-        @pl.when(block // per != z)
-        def _():
-            p_copy(block).start()
+        return dot(attn_ref[...], wall[block], 1, 0)
+
+    def tick(now):
+        for way in range(2):
+            slots = right_ref if way == 0 else left_ref
+            place = z if way == 0 else nhead - 1 - z
+            i = now - place * LAG
+
+            @pl.when((i >= 0) & (i < nseq))
+            def _():
+                block = block_at(i)
+                owner = block // per
+
+                @pl.when(owner > z if way == 0 else owner < z)
+                def _():
+                    @pl.when(place > 0)
+                    def _():
+                        hop_copy(way, block).wait_recv()
+                        slots[block] = (project(block) + slots[block].astype(F32)).astype(BF16)
+
+                    @pl.when(place == 0)
+                    def _():
+                        slots[block] = project(block).astype(BF16)
+
+                    hop_copy(way, block).start()
+
+    def ticks(first, last):
+        def step(now, carry):
+            tick(now)
+            return carry
+
+        lax.fori_loop(first, last, step, 0)
 
     own_w.wait()
-    project(me)
+    tick(0)
     w_wait(partner)
-    project(partner)
+    tick(1)
     for delta in range(1, chips):
         base = ((chip - delta + chips) % chips) * 2
         w_wait(base + core)
         w_to_partner(delta).start()
         if delta < nhead - 1:
             u_arrived(delta)
-        project(base + core)
+        tick(2 * delta)
         w_wait(base + 1 - core)
-        project(base + 1 - core)
+        tick(2 * delta + 1)
 
     def grad_product(block):
         for sub in range(per):
@@ -246,6 +291,8 @@
     acc[...] = jnp.zeros_like(acc)
     grad_product(z)
     for hop in range(1, nhead):
+        if hop == nhead - 1:
+            ticks(nseq, nseq + LAG)
         if hop >= min(chips, nhead - 1):
             u_arrived(hop)
         for way in range(2):
@@ -277,7 +324,12 @@
         gm_own[h, hd:] = jnp.where(row == 0, norm, 0.0).astype(BF16)
 
     for d in range(1, span):
-        gm_copy(d).start()
+
+        @pl.when(me >= d)
+        def _():
+            gm_copy(d).start()
+
+    ticks(nseq + LAG, nseq + (nhead - 2) * LAG)
 
     @over_heads
     def _(h):
@@ -298,7 +350,14 @@
         ).astype(BF16)
 
     for d in range(1, span):
-        gm_copy(d).wait_recv()
+
+        @pl.when(me + d < nseq)
+        def _():
+            gm_copy(d).wait_recv()
+
+        @pl.when(me + d >= nseq)
+        def _():
+            gm_in[d - 1] = jnp.zeros(gm_in.shape[1:], BF16)
 
     @over_heads
     def _(h):
@@ -312,25 +371,40 @@
             dv_ref[:, lanes(h)] + dot(lifted, total[:hd], 1, 1)
         ).astype(BF16)
 
-    for step in range(1, nhead):
-        other = (z + step) % nhead
-        for sub in range(per):
-            remote(
-                terms.at[sub], parts.at[other, sub], p_send.at[sub], p_recv.at[other, sub], me,
-                other,
-            ).wait_recv()
     for sub in range(per):
-        total = terms[z * per + sub].astype(F32)
-        for step in range(1, nhead):
-            total = total + parts[(z + step) % nhead, sub].astype(F32)
-        mixed_ref[:, sub * wcols:(sub + 1) * wcols] = total.astype(BF16)
-
-    for step in range(1, nhead):
-        for sub in range(per):
-            p_copy(((z + step) % nhead) * per + sub).wait_send()
+        cols = slice(sub * wcols, (sub + 1) * wcols)
+        block = z * per + sub
+        acc[:, cols] = project(block)
+        for way in range(2):
+            slots = right_ref if way == 0 else left_ref
+
+            @pl.when(has_left if way == 0 else has_right)
+            def _():
+                hop_copy(way, block).wait_recv()
+                acc[:, cols] += slots[block].astype(F32)
+
+        mixed_ref[:, cols] = acc[:, cols].astype(BF16)
+
+    def sent(block, carry):
+        for way in range(2):
+
+            @pl.when(block // per > z if way == 0 else block // per < z)
+            def _():
+                hop_copy(way, block).wait_send()
+
+        return carry
+
+    lax.fori_loop(0, nseq, sent, 0)
     for d in range(1, span):
-        kv_copy(d).wait_send()
-        gm_copy(d).wait_send()
+
+        @pl.when(me + d < nseq)
+        def _():
+            kv_copy(d).wait_send()
+
+        @pl.when(me >= d)
+        def _():
+            gm_copy(d).wait_send()
+
     for delta in range(chips):
         w_to_partner(delta).wait_send()
         if delta > 0:
@@ -364,7 +438,7 @@
             pltpu.VMEM((nseq, width, wcols), BF16),
             pltpu.VMEM((nhead, seg, wcols * per), BF16),
             pltpu.VMEM((nseq, seg, wcols), BF16),
-            pltpu.VMEM((nhead, per, seg, wcols), BF16),
+            pltpu.VMEM((nseq, seg, wcols), BF16),
             pltpu.VMEM((heads, seg, seg), BF16),
             pltpu.VMEM((seg, width), F32),
             pltpu.VMEM((seg, width), BF16),
@@ -382,7 +456,7 @@
             dma((span,)), dma((span,)), dma((nseq,)),
             dma((2, nhead)), dma((nhead,)),
             dma((span - 1,)), dma((span - 1,)), dma((span - 1,)), dma((span - 1,)),
-            dma((nseq,)), dma((nhead, per)), dma((2,)),
+            dma((2, nseq)), dma((2, nseq)), dma((2,)),
         ],
         compiler_params=pltpu.CompilerParams(
             collective_id=0, has_side_effects=True, vmem_limit_bytes=60 * 1024 * 1024

time: 222 us -> 160 us (0.72)
  Pallas kernels: 215 us -> 151 us
    pallas_call x1, Pallas kernels: 215 us -> 151 us  [per_device(): pl.pallas_call(functools.partial(kernel, nseq, nhead, heads), out_shape=[...]
where the time goes in v2:
time: 160 us; the launch traced here: 158 us
  Pallas kernels  151 us (94%)
  local copies, waits for them, and re-layouts  6.53 us (4%)
    pallas_call x1, Pallas kernels, per_device(): pl.pallas_call(functools.partial(kernel, nseq, nhead, heads), out_shape=[...  151 us
    unnamed x10, local copies, waits for them, and re-layouts  6.53 us

profile of v2, /device:TPU:7, one launch (start us, length us, event | category | flops | bytes accessed | tf_op | source)
XLA Modules:
  0.0 158.0 jit_solution(2403958411543302175)
XLA Ops:
  0.6 150.9 %layer.1 = (bf16[512,1024]{1,0:T(8,128)(2,1)}, bf16[512,1024]{1,0:T(8,128)(2,1)}, bf16[512,1024]{1,0:T(8,128)(2,1)}, bf16[512,1024]{1,0:T(8,128)(2,1)}) custom-call(s32[8]{0:T(128)} %valid_ref.1, s32[8]{0:T(128)} %doc_ref.1, f32[8]{0:T(128)} %gate_ref.1, bf16[512,1024]{1,0:T(8,128)(2,1)} %q_ref.1, bf16[512,1024]{1,0:T(8,128)(2,1)} %k_ref.1, ...), custom_call_target="tpu_custom_call" | custom-call | flops 8589934592 | bytes 9437184 | tf_op jit(solution)/shard_map/layer/pallas_call | solution.py:432
  151.5 0.0 copy-start.2
  151.5 2.4 %copy.16 = bf16[512,1024]{1,0:T(8,128)(2,1)} copy(bf16[512,1024]{1,0:T(8,128)(2,1)} %get-tuple-element.8) | data formatting | bytes 2097152
  153.9 0.0 copy-done.2
  153.9 0.0 copy-start.1
  153.9 1.0 copy.17
  154.8 0.6 copy-done.1
  155.5 0.0 copy-start
  155.5 1.0 copy.18
  156.4 0.6 copy-done
  157.1 1.0 copy.19
Async XLA Ops:
  151.5 2.4 %copy-start.2 = (bf16[512,1024]{1,0:T(8,128)(2,1)S(1)}, bf16[512,1024]{1,0:T(8,128)(2,1)}, u32[]{:S(2)}) copy-start(bf16[512,1024]{1,0:T(8,128)(2,1)} %get-tuple-element.9) | copy-start | bytes 3145732
  153.9 1.6 %copy-start.1 = (bf16[512,1024]{1,0:T(8,128)(2,1)S(1)}, bf16[512,1024]{1,0:T(8,128)(2,1)}, u32[]{:S(2)}) copy-start(bf16[512,1024]{1,0:T(8,128)(2,1)} %get-tuple-element.10) | copy-start | bytes 3145732
  155.5 1.6 %copy-start = (bf16[512,1024]{1,0:T(8,128)(2,1)S(1)}, bf16[512,1024]{1,0:T(8,128)(2,1)}, u32[]{:S(2)}) copy-start(bf16[512,1024]{1,0:T(8,128)(2,1)} %get-tuple-element.11) | copy-start | bytes 3145732

commit v3 on v2

--- a/solution.py
+++ b/solution.py
@@ -267,6 +267,8 @@
 
         lax.fori_loop(first, last, step, 0)
 
+    if nhead > 2:
+        u_arrived(1)
     own_w.wait()
     tick(0)
     w_wait(partner)
@@ -275,11 +277,11 @@
         base = ((chip - delta + chips) % chips) * 2
         w_wait(base + core)
         w_to_partner(delta).start()
-        if delta < nhead - 1:
-            u_arrived(delta)
         tick(2 * delta)
         w_wait(base + 1 - core)
         tick(2 * delta + 1)
+        if delta + 1 < nhead - 1:
+            u_arrived(delta + 1)
 
     def grad_product(block):
         for sub in range(per):
@@ -293,7 +295,7 @@
     for hop in range(1, nhead):
         if hop == nhead - 1:
             ticks(nseq, nseq + LAG)
-        if hop >= min(chips, nhead - 1):
+        if hop > chips or hop == nhead - 1:
             u_arrived(hop)
         for way in range(2):
             there = (z >= hop) if way == 0 else (z + hop <= nhead - 1)

time: 160 us -> 151 us (0.944)
  the two profiles are of different devices: /device:TPU:7 before, /device:TPU:10 now
where the time goes in v3:
time: 151 us; the launch traced here: 150 us
  Pallas kernels  143 us (95%)
  local copies, waits for them, and re-layouts  6.53 us (4%)
    pallas_call x1, Pallas kernels, per_device(): pl.pallas_call(functools.partial(kernel, nseq, nhead, heads), out_shape=[...  143 us
    unnamed x10, local copies, waits for them, and re-layouts  6.53 us

profile of v3, /device:TPU:10, one launch (start us, length us, event | category | flops | bytes accessed | tf_op | source)
XLA Modules:
  0.0 150.3 jit_solution(5006226315832923122)
XLA Ops:
  0.6 143.1 %layer.1 = (bf16[512,1024]{1,0:T(8,128)(2,1)}, bf16[512,1024]{1,0:T(8,128)(2,1)}, bf16[512,1024]{1,0:T(8,128)(2,1)}, bf16[512,1024]{1,0:T(8,128)(2,1)}) custom-call(s32[8]{0:T(128)} %valid_ref.1, s32[8]{0:T(128)} %doc_ref.1, f32[8]{0:T(128)} %gate_ref.1, bf16[512,1024]{1,0:T(8,128)(2,1)} %q_ref.1, bf16[512,1024]{1,0:T(8,128)(2,1)} %k_ref.1, ...), custom_call_target="tpu_custom_call" | custom-call | flops 8589934592 | bytes 9437184 | tf_op jit(solution)/shard_map/layer/pallas_call | solution.py:434
  143.8 0.0 copy-start.2
  143.8 2.4 %copy.16 = bf16[512,1024]{1,0:T(8,128)(2,1)} copy(bf16[512,1024]{1,0:T(8,128)(2,1)} %get-tuple-element.8) | data formatting | bytes 2097152
  146.1 0.0 copy-done.2
  146.1 0.0 copy-start.1
  146.1 1.0 copy.17
  147.1 0.6 copy-done.1
  147.7 0.0 copy-start
  147.7 1.0 copy.18
  148.7 0.6 copy-done
  149.4 1.0 copy.19
Async XLA Ops:
  143.8 2.4 %copy-start.2 = (bf16[512,1024]{1,0:T(8,128)(2,1)S(1)}, bf16[512,1024]{1,0:T(8,128)(2,1)}, u32[]{:S(2)}) copy-start(bf16[512,1024]{1,0:T(8,128)(2,1)} %get-tuple-element.9) | copy-start | bytes 3145732
  146.1 1.6 %copy-start.1 = (bf16[512,1024]{1,0:T(8,128)(2,1)S(1)}, bf16[512,1024]{1,0:T(8,128)(2,1)}, u32[]{:S(2)}) copy-start(bf16[512,1024]{1,0:T(8,128)(2,1)} %get-tuple-element.10) | copy-start | bytes 3145732
  147.7 1.6 %copy-start = (bf16[512,1024]{1,0:T(8,128)(2,1)S(1)}, bf16[512,1024]{1,0:T(8,128)(2,1)}, u32[]{:S(2)}) copy-start(bf16[512,1024]{1,0:T(8,128)(2,1)} %get-tuple-element.11) | copy-start | bytes 3145732
